TPU v7x, 32 devices: a whole 2x2x4 slice. The times are simulated.
32 devices in a mesh: lon: 16 (over z, y, core), lat: 2 (over x).
Axes of the slice: x: 2, y: 2, z: 4, core: 2. Of those that a mesh axis runs over, the one named last changes fastest.
Arguments:
- concentration: float32 [128, 448, 128], P('lon', 'lat'), may hold values from -6 to 6
- wind: bfloat16 [3, 128, 448, 128], P(None, 'lon', 'lat'), may hold values from -0.099609375 to 0.099609375
- kappa: bfloat16 [128, 448, 128], P('lon', 'lat'), may hold values from 0.0099487305 to 0.059814453
- observed: bfloat16 [128, 448, 128], P('lon', 'lat'), may hold values from -6 to 6
Outputs:
- grad_conc: float32 [128, 448, 128], P('lon', 'lat')
- grad_kappa: float32 [128, 448, 128], P('lon', 'lat')
All inputs are finite; a program needn't handle non-finite values.
Results may differ from a plain program's by a relative error of at most 0.0023.
Values may be sent and summed in bfloat16 or wider, within the bound.
A program may use at most 128 MiB of HBM per device.

v0:
```python
import jax
import jax.numpy as jnp
from jax import lax
from jax.sharding import PartitionSpec as P


def for_sending(array):

    def short(part):
        return part.astype(jnp.bfloat16) if part.dtype == jnp.float32 else part

    return jax.tree.map(short, array)


def passed_along(value, axis, steps):
    count = lax.axis_size(axis)
    pairs = [(source, (source + steps) % count) for source in range(count)]
    return lax.ppermute(value, axis, pairs)


def passed_along_2(value, axis, steps):
    count = lax.axis_size(axis)
    leading, last = (max(0, -steps), min(count, count - steps))
    return lax.ppermute(value, axis, [(source, source + steps) for source in range(leading, last)])


def coefs(speed, diffuse, opened):
    return (
        (jnp.maximum(speed, 0.0) + diffuse) * opened,
        (jnp.minimum(speed, 0.0) - diffuse) * opened,
    )


def level_next(field):
    return jnp.concatenate([field[:, :, 1:], jnp.zeros_like(field[:, :, :1])], 2)


def level_west(field):
    return jnp.concatenate([jnp.zeros_like(field[:, :, :1]), field[:, :, :-1]], 2)


def advance_faces(conc, table):
    rim_lon = passed_along(for_sending(conc[0:1]), "lon", -1)
    rim_lat = passed_along_2(conc[:, 0:1], "lat", -1)
    nexts = (
        jnp.concatenate([conc[1:], rim_lon], 0),
        jnp.concatenate([conc[:, 1:], rim_lat], 1),
        level_next(conc),
    )
    fluxes = tuple((pair[0] * conc + pair[1] * nearby for pair, nearby in zip(table, nexts)))
    back_lon = passed_along(for_sending(fluxes[0][-1:]), "lon", 1)
    back_lat = passed_along_2(fluxes[1][:, -1:], "lat", 1)
    west_lon = jnp.concatenate([back_lon, fluxes[0][:-1]], 0)
    west_lat = jnp.concatenate([back_lat, fluxes[1][:, :-1]], 1)
    west_level = level_west(fluxes[2])
    return (conc - (fluxes[0] + fluxes[1] + fluxes[2]) + (west_lon + west_lat + west_level), nexts)


def retreat_faces(adjoint, table):
    rim_lon = passed_along(for_sending(adjoint[0:1]), "lon", -1)
    rim_lat = passed_along_2(adjoint[:, 0:1], "lat", -1)
    gaps = (
        jnp.concatenate([adjoint[1:], rim_lon], 0) - adjoint,
        jnp.concatenate([adjoint[:, 1:], rim_lat], 1) - adjoint,
        level_next(adjoint) - adjoint,
    )
    parts = tuple((pair[1] * gap for pair, gap in zip(table, gaps)))
    back_lon = passed_along(for_sending(parts[0][-1:]), "lon", 1)
    back_lat = passed_along_2(parts[1][:, -1:], "lat", 1)
    west_lon = jnp.concatenate([back_lon, parts[0][:-1]], 0)
    west_lat = jnp.concatenate([back_lat, parts[1][:, :-1]], 1)
    west_level = level_west(parts[2])
    gained = table[0][0] * gaps[0] + table[1][0] * gaps[1] + table[2][0] * gaps[2]
    return (adjoint + gained + (west_lon + west_lat + west_level), gaps)


def kappa_term(gaps, conc, nexts, north_open, upper_open):
    return (
        gaps[0] * (conc - nexts[0])
        + gaps[1] * (conc - nexts[1]) * north_open
        + gaps[2] * (conc - nexts[2]) * upper_open
    )


def body(concentration, wind, kappa, observed):
    lat_rows = concentration.shape[1]
    levels = concentration.shape[2]
    upper_open = (lax.broadcasted_iota(jnp.int32, (1, 1, levels), 2) < levels - 1).astype(
        jnp.float32
    )
    lat_place = lax.axis_index("lat") * lat_rows + lax.broadcasted_iota(
        jnp.int32, (1, lat_rows, 1), 1
    )
    north_open = (lat_place < lat_rows * lax.axis_size("lat") - 1).astype(jnp.float32)
    speeds = wind.astype(jnp.float32)
    diffuse = kappa.astype(jnp.float32)
    table = (
        coefs(speeds[0], diffuse, 1.0),
        coefs(speeds[1], diffuse, north_open),
        coefs(speeds[2], diffuse, upper_open),
    )
    middle, nexts_first = advance_faces(concentration, table)
    final, nexts_second = advance_faces(middle, table)
    adjoint = final - observed.astype(jnp.float32)
    adjoint, gaps = retreat_faces(adjoint, table)
    grad_kappa = kappa_term(gaps, middle, nexts_second, north_open, upper_open)
    grad_conc, gaps = retreat_faces(adjoint, table)
    grad_kappa = grad_kappa + kappa_term(gaps, concentration, nexts_first, north_open, upper_open)
    return (grad_conc, grad_kappa)


def solution(mesh):
    return jax.shard_map(
        body,
        mesh=mesh,
        in_specs=(
            P("lon", "lat", None),
            P(None, "lon", "lat", None),
            P("lon", "lat", None),
            P("lon", "lat", None),
        ),
        out_specs=(P("lon", "lat", None), P("lon", "lat", None)),
        check_vma=False,
    )
```

profile of v0, /device:TPU:0, one launch (start us, length us, event | category | flops | bytes accessed | tf_op | source)
XLA Modules:
  0.0 68.7 jit_solution(7764781376442786179)
XLA Ops:
  0.7 0.9 %slice.142 = f32[8,1,128]{2,1,0:T(1,128)S(1)} slice(f32[8,224,128]{2,1,0:T(8,128)} %param.4), slice={[0:8], [0:1], [0:128]} | slice | bytes 8192 | tf_op jit(solution)/shard_map/slice | solution.py:44
  1.6 1.3 %collective-permute-start.1 = (f32[8,1,128]{2,1,0:T(1,128)S(1)}, f32[8,1,128]{2,1,0:T(1,128)S(1)}, u32[]{:S(2)}, u32[]{:S(2)}) collective-permute-start(f32[8,1,128]{2,1,0:T(1,128)S(1)} %slice.142), channel_id=1, source_target_pairs={{1,0},{3,2},{5,4},{7,6},{9,8},{11,10},{13,12},{15,14},{17,16},{19,... | collective-permute-start | bytes 12296 | tf_op jit(solution)/shard_map/ppermute | solution.py:24
  2.9 0.9 %slice.286 = bf16[1,224,128]{2,1,0:T(8,128)(2,1)S(1)} slice(f32[8,224,128]{2,1,0:T(8,128)} %param.4), slice={[0:1], [0:224], [0:128]} | slice | bytes 114688 | tf_op jit(solution)/shard_map/slice | solution.py:43
  3.8 5.4 %collective-permute-start = (bf16[1,224,128]{2,1,0:T(8,128)(2,1)S(1)}, bf16[1,224,128]{2,1,0:T(8,128)(2,1)S(1)}, u32[]{:S(2)}, u32[]{:S(2)}) collective-permute-start(bf16[1,224,128]{2,1,0:T(8,128)(2,1)S(1)} %slice.286), channel_id=1, source_target_pairs={{0,30},{2,0},{4,2},{6,4},{8,6},{10,8},{12,10},{14,12},{16,14},{18,... | collective-permute-start | bytes 172040 | tf_op jit(solution)/shard_map/ppermute | solution.py:18
  9.2 1.2 %slice.138 = f32[7,224,128]{2,1,0:T(8,128)S(1)} slice(f32[8,224,128]{2,1,0:T(8,128)} %param.4), slice={[1:8], [0:224], [0:128]} | slice | bytes 1605632 | tf_op jit(solution)/shard_map/slice | solution.py:46
  10.4 1.2 %slice.141 = f32[8,223,128]{2,1,0:T(8,128)S(1)} slice(f32[8,224,128]{2,1,0:T(8,128)} %param.4), slice={[0:8], [1:224], [0:128]} | slice | bytes 1826816 | tf_op jit(solution)/shard_map/slice | solution.py:47
  11.7 0.3 slice.144
  12.0 0.3 convert_element_type.63
  12.3 0.4 copy-done.1
  12.7 0.8 %multiply_add_fusion.3 = (f32[8,224,128]{2,1,0:T(8,128)S(1)}, f32[8,224,128]{2,1,0:T(8,128)S(1)}, f32[8,224,128]{2,1,0:T(8,128)S(1)}, f32[8,224,128]{2,1,0:T(8,128)S(1)}) fusion(f32[8,224,128]{2,1,0:T(8,128)S(1)} %copy-done, f32[8,224,127]{2,1,0:T(8,128)S(1)} %slice.144, f32[128]{0:T(128)S(1)} %compare_convert_fusion, bf16[8,224,128]{2,1,0:T(8,128)(2,1)S(1)} %copy-done.1, ...), kind=kLoop, calls=%fused_computation.39 | loop fusion | flops 6422528 | bytes 10545536 | tf_op jit(solution)/shard_map/add | solution.py:50
  13.5 0.1 collective-permute-start.2
  13.6 4.3 %collective-permute-start.3 = (f32[8,1,128]{2,1,0:T(1,128)S(1)}, f32[8,1,128]{2,1,0:T(1,128)S(1)}, u32[]{:S(2)}, u32[]{:S(2)}) collective-permute-start(f32[8,1,128]{2,1,0:T(1,128)S(1)} %slice.186), channel_id=1, source_target_pairs={{0,1},{2,3},{4,5},{6,7},{8,9},{10,11},{12,13},{14,15},{16,17},{18,... | collective-permute-start | bytes 12296 | tf_op jit(solution)/shard_map/ppermute | solution.py:24
  18.0 1.9 %collective-permute-done.2 = bf16[1,224,128]{2,1,0:T(8,128)(2,1)S(1)} collective-permute-done((bf16[1,224,128]{2,1,0:T(8,128)(2,1)S(1)}, bf16[1,224,128]{2,1,0:T(8,128)(2,1)S(1)}, u32[]{:S(2)}, u32[]{:S(2)}) %collective-permute-start.2) | collective-permute-done | bytes 57376 | tf_op jit(solution)/shard_map/ppermute | solution.py:18
  19.9 0.7 fusion.5
  20.6 2.9 %collective-permute-start.4 = (bf16[1,224,128]{2,1,0:T(8,128)(2,1)S(1)}, bf16[1,224,128]{2,1,0:T(8,128)(2,1)S(1)}, u32[]{:S(2)}, u32[]{:S(2)}) collective-permute-start(bf16[1,224,128]{2,1,0:T(8,128)(2,1)S(1)} %slice.284), channel_id=1, source_target_pairs={{0,30},{2,0},{4,2},{6,4},{8,6},{10,8},{12,10},{14,12},{16,14},{18,... | collective-permute-start | bytes 172040 | tf_op jit(solution)/shard_map/ppermute | solution.py:18
  23.5 1.3 %collective-permute-start.5 = (f32[8,1,128]{2,1,0:T(1,128)S(1)}, f32[8,1,128]{2,1,0:T(1,128)S(1)}, u32[]{:S(2)}, u32[]{:S(2)}) collective-permute-start(f32[8,1,128]{2,1,0:T(1,128)S(1)} %slice.192), channel_id=1, source_target_pairs={{1,0},{3,2},{5,4},{7,6},{9,8},{11,10},{13,12},{15,14},{17,16},{19,... | collective-permute-start | bytes 12296 | tf_op jit(solution)/shard_map/ppermute | solution.py:24
  24.9 0.3 slice.193
  25.2 0.1 slice.191
  25.2 0.1 collective-permute-done.4
  25.4 3.7 %collective-permute-done.5 = f32[8,1,128]{2,1,0:T(1,128)S(1)} collective-permute-done((f32[8,1,128]{2,1,0:T(1,128)S(1)}, f32[8,1,128]{2,1,0:T(1,128)S(1)}, u32[]{:S(2)}, u32[]{:S(2)}) %collective-permute-start.5) | collective-permute-done | bytes 4128 | tf_op jit(solution)/shard_map/ppermute | solution.py:24
  29.0 0.8 %multiply_add_fusion = (f32[8,224,128]{2,1,0:T(8,128)S(1)}, f32[8,224,128]{2,1,0:T(8,128)S(1)}, f32[8,224,128]{2,1,0:T(8,128)S(1)}) fusion(f32[8,224,128]{2,1,0:T(8,128)S(1)} %get-tuple-element.3, f32[8,224,128]{2,1,0:T(8,128)S(1)} %fusion.5, f32[8,224,127]{2,1,0:T(8,128)S(1)} %slice.193, f32[128]{0:T(128)S(1)} %compare_convert_fusion, ...), kind=kLoop, calls=%fused_computation.36 | loop fusion | flops 5734400 | bytes 10545536 | tf_op jit(solution)/shard_map/add | solution.py:50
  29.9 0.1 collective-permute-start.6
  30.0 1.6 %collective-permute-start.7 = (f32[8,1,128]{2,1,0:T(1,128)S(1)}, f32[8,1,128]{2,1,0:T(1,128)S(1)}, u32[]{:S(2)}, u32[]{:S(2)}) collective-permute-start(f32[8,1,128]{2,1,0:T(1,128)S(1)} %slice.196), channel_id=1, source_target_pairs={{0,1},{2,3},{4,5},{6,7},{8,9},{10,11},{12,13},{14,15},{16,17},{18,... | collective-permute-start | bytes 12296 | tf_op jit(solution)/shard_map/ppermute | solution.py:24
  31.7 4.7 %collective-permute-done.6 = bf16[1,224,128]{2,1,0:T(8,128)(2,1)S(1)} collective-permute-done((bf16[1,224,128]{2,1,0:T(8,128)(2,1)S(1)}, bf16[1,224,128]{2,1,0:T(8,128)(2,1)S(1)}, u32[]{:S(2)}, u32[]{:S(2)}) %collective-permute-start.6) | collective-permute-done | bytes 57376 | tf_op jit(solution)/shard_map/ppermute | solution.py:18
  36.4 0.7 %fusion.8 = f32[8,224,128]{2,1,0:T(8,128)S(1)} fusion(f32[7,224,128]{2,1,0:T(8,128)S(1)} %slice.195, f32[1,224,128]{2,1,0:T(8,128)S(1)} %convert_element_type.70, f32[8,223,128]{2,1,0:T(8,128)S(1)} %bitcast.59, f32[8,1,128]{2,1,0:T(1,128)S(1)} %collective-permute-done.7, bf16[8,224,128]{2,1,0:T(8,128)(2,1)S(1)} %copy-done.3, f32[8,224,127]{2,1,0:T(8,128)S(1)} %bitcast.61, ...), kind=kLoop, calls=%fused_computation.22 | loop fusion | flops 2293760 | bytes 7791616 | tf_op jit(solution)/shard_map/sub | solution.py:104
  37.1 0.2 collective-permute-start.8
  37.3 1.3 %collective-permute-start.9 = (f32[8,1,128]{2,1,0:T(1,128)S(1)}, f32[8,1,128]{2,1,0:T(1,128)S(1)}, u32[]{:S(2)}, u32[]{:S(2)}) collective-permute-start(f32[8,1,128]{2,1,0:T(1,128)S(1)} %slice.202), channel_id=1, source_target_pairs={{1,0},{3,2},{5,4},{7,6},{9,8},{11,10},{13,12},{15,14},{17,16},{19,... | collective-permute-start | bytes 12296 | tf_op jit(solution)/shard_map/ppermute | solution.py:24
  38.6 0.3 slice.203
  38.9 0.1 slice.201
  39.0 0.1 collective-permute-done.8
  39.1 3.7 %collective-permute-done.9 = f32[8,1,128]{2,1,0:T(1,128)S(1)} collective-permute-done((f32[8,1,128]{2,1,0:T(1,128)S(1)}, f32[8,1,128]{2,1,0:T(1,128)S(1)}, u32[]{:S(2)}, u32[]{:S(2)}) %collective-permute-start.9) | collective-permute-done | bytes 4128 | tf_op jit(solution)/shard_map/ppermute | solution.py:24
  42.8 0.5 fusion.16
  43.3 1.7 %collective-permute-start.11 = (f32[8,1,128]{2,1,0:T(1,128)S(1)}, f32[8,1,128]{2,1,0:T(1,128)S(1)}, u32[]{:S(2)}, u32[]{:S(2)}) collective-permute-start(f32[8,1,128]{2,1,0:T(1,128)S(1)} %slice.206), channel_id=1, source_target_pairs={{0,1},{2,3},{4,5},{6,7},{8,9},{10,11},{12,13},{14,15},{16,17},{18,... | collective-permute-start | bytes 12296 | tf_op jit(solution)/shard_map/ppermute | solution.py:24
  45.0 0.1 collective-permute-start.10
  45.1 0.1 slice_multiply_fusion.1
  45.2 6.2 %collective-permute-done.10 = bf16[1,224,128]{2,1,0:T(8,128)(2,1)S(1)} collective-permute-done((bf16[1,224,128]{2,1,0:T(8,128)(2,1)S(1)}, bf16[1,224,128]{2,1,0:T(8,128)(2,1)S(1)}, u32[]{:S(2)}, u32[]{:S(2)}) %collective-permute-start.10) | collective-permute-done | bytes 57376 | tf_op jit(solution)/shard_map/ppermute | solution.py:18
  51.5 1.1 %fusion.10 = f32[8,224,128]{2,1,0:T(8,128)S(1)} fusion(f32[7,224,128]{2,1,0:T(8,128)S(1)} %slice.205, f32[1,224,128]{2,1,0:T(8,128)S(1)} %convert_element_type.73, f32[8,223,128]{2,1,0:T(8,128)S(1)} %bitcast.64, f32[8,1,128]{2,1,0:T(1,128)S(1)} %collective-permute-done.11, f32[8,224,127]{2,1,0:T(8,128)S(1)} %slice_multiply_fusion.1, ...), kind=kLoop, calls=%fused_computation.27 | loop fusion | flops 5734400 | bytes 10538368 | tf_op jit(solution)/shard_map/add | solution.py:74
  52.6 1.3 %collective-permute-start.13 = (f32[8,1,128]{2,1,0:T(1,128)S(1)}, f32[8,1,128]{2,1,0:T(1,128)S(1)}, u32[]{:S(2)}, u32[]{:S(2)}) collective-permute-start(f32[8,1,128]{2,1,0:T(1,128)S(1)} %slice.213), channel_id=1, source_target_pairs={{1,0},{3,2},{5,4},{7,6},{9,8},{11,10},{13,12},{15,14},{17,16},{19,... | collective-permute-start | bytes 12296 | tf_op jit(solution)/shard_map/ppermute | solution.py:24
  54.0 0.3 slice.214
  54.3 0.1 slice.212
  54.4 0.1 collective-permute-done.12
  54.5 3.7 %collective-permute-done.13 = f32[8,1,128]{2,1,0:T(1,128)S(1)} collective-permute-done((f32[8,1,128]{2,1,0:T(1,128)S(1)}, f32[8,1,128]{2,1,0:T(1,128)S(1)}, u32[]{:S(2)}, u32[]{:S(2)}) %collective-permute-start.13) | collective-permute-done | bytes 4128 | tf_op jit(solution)/shard_map/ppermute | solution.py:24
  58.1 0.5 fusion.15
  58.7 1.7 %collective-permute-start.15 = (f32[8,1,128]{2,1,0:T(1,128)S(1)}, f32[8,1,128]{2,1,0:T(1,128)S(1)}, u32[]{:S(2)}, u32[]{:S(2)}) collective-permute-start(f32[8,1,128]{2,1,0:T(1,128)S(1)} %slice.217), channel_id=1, source_target_pairs={{0,1},{2,3},{4,5},{6,7},{8,9},{10,11},{12,13},{14,15},{16,17},{18,... | collective-permute-start | bytes 12296 | tf_op jit(solution)/shard_map/ppermute | solution.py:24
  60.4 3.1 %add_add_fusion = f32[8,224,128]{2,1,0:T(8,128)} fusion(f32[8,224,128]{2,1,0:T(8,128)S(1)} %copy-done, f32[8,224,128]{2,1,0:T(8,128)S(1)} %fusion.5, f32[8,224,127]{2,1,0:T(8,128)S(1)} %slice.193, f32[8,224,127]{2,1,0:T(8,128)S(1)} %slice.144, f32[1,224,128]{2,1,0:T(8,128)S(1)} %convert_element_type.69, f32[7,224,128]{2,1,0:T(8,128)S(1)} %slice.189, ...), kind=kLoop, calls=%fused_computation.33 | loop fusion | flops 8028160 | bytes 15570304 | tf_op jit(solution)/shard_map/add | solution.py:108
  63.6 0.1 slice_multiply_fusion
  63.8 3.0 %collective-permute-done.14 = bf16[1,224,128]{2,1,0:T(8,128)(2,1)S(1)} collective-permute-done((bf16[1,224,128]{2,1,0:T(8,128)(2,1)S(1)}, bf16[1,224,128]{2,1,0:T(8,128)(2,1)S(1)}, u32[]{:S(2)}, u32[]{:S(2)}) %collective-permute-start.14) | collective-permute-done | bytes 57376 | tf_op jit(solution)/shard_map/ppermute | solution.py:18
  66.7 2.0 %fusion.12 = f32[8,224,128]{2,1,0:T(8,128)} fusion(f32[7,224,128]{2,1,0:T(8,128)S(1)} %slice.216, f32[1,224,128]{2,1,0:T(8,128)S(1)} %convert_element_type.75, f32[8,223,128]{2,1,0:T(8,128)S(1)} %bitcast.63, f32[8,1,128]{2,1,0:T(1,128)S(1)} %collective-permute-done.15, f32[8,224,127]{2,1,0:T(8,128)S(1)} %slice_multiply_fusion, ...), kind=kLoop, calls=%fused_computation.32 | loop fusion | flops 5734400 | bytes 10538368 | tf_op jit(solution)/shard_map/add | solution.py:74
  (46 shorter events, 0.7 us)
Async XLA Ops:
  0.6 11.0 %copy-start = (f32[8,224,128]{2,1,0:T(8,128)S(1)}, f32[8,224,128]{2,1,0:T(8,128)}, u32[]{:S(2)}) copy-start(f32[8,224,128]{2,1,0:T(8,128)} %param.4) | copy-start | bytes 2752516
  0.6 11.3 %copy-start.2 = (bf16[3,8,224,128]{3,2,1,0:T(8,128)(2,1)S(1)}, bf16[3,8,224,128]{3,2,1,0:T(8,128)(2,1)}, u32[]{:S(2)}) copy-start(bf16[3,8,224,128]{3,2,1,0:T(8,128)(2,1)} %param.5) | copy-start | bytes 4128772
  1.6 10.8 %collective-permute-start.1 = (f32[8,1,128]{2,1,0:T(1,128)S(1)}, f32[8,1,128]{2,1,0:T(1,128)S(1)}, u32[]{:S(2)}, u32[]{:S(2)}) collective-permute-start(f32[8,1,128]{2,1,0:T(1,128)S(1)} %slice.142), channel_id=1, source_target_pairs={{1,0},{3,2},{5,4},{7,6},{9,8},{11,10},{13,12},{15,14},{17,16},{19,... | collective-permute-start | bytes 12296 | tf_op jit(solution)/shard_map/ppermute | solution.py:24
  3.8 8.5 %collective-permute-start = (bf16[1,224,128]{2,1,0:T(8,128)(2,1)S(1)}, bf16[1,224,128]{2,1,0:T(8,128)(2,1)S(1)}, u32[]{:S(2)}, u32[]{:S(2)}) collective-permute-start(bf16[1,224,128]{2,1,0:T(8,128)(2,1)S(1)} %slice.286), channel_id=1, source_target_pairs={{0,30},{2,0},{4,2},{6,4},{8,6},{10,8},{12,10},{14,12},{16,14},{18,... | collective-permute-start | bytes 172040 | tf_op jit(solution)/shard_map/ppermute | solution.py:18
  11.7 1.0 %copy-start.1 = (bf16[8,224,128]{2,1,0:T(8,128)(2,1)S(1)}, bf16[8,224,128]{2,1,0:T(8,128)(2,1)}, u32[]{:S(2)}) copy-start(bf16[8,224,128]{2,1,0:T(8,128)(2,1)} %param.6) | copy-start | bytes 1376260
  13.5 6.4 %collective-permute-start.2 = (bf16[1,224,128]{2,1,0:T(8,128)(2,1)S(1)}, bf16[1,224,128]{2,1,0:T(8,128)(2,1)S(1)}, u32[]{:S(2)}, u32[]{:S(2)}) collective-permute-start(bf16[1,224,128]{2,1,0:T(8,128)(2,1)S(1)} %slice.285), channel_id=1, source_target_pairs={{0,2},{2,4},{4,6},{6,8},{8,10},{10,12},{12,14},{14,16},{16,18},{18... | collective-permute-start | bytes 172040 | tf_op jit(solution)/shard_map/ppermute | solution.py:18
  13.6 6.3 %collective-permute-start.3 = (f32[8,1,128]{2,1,0:T(1,128)S(1)}, f32[8,1,128]{2,1,0:T(1,128)S(1)}, u32[]{:S(2)}, u32[]{:S(2)}) collective-permute-start(f32[8,1,128]{2,1,0:T(1,128)S(1)} %slice.186), channel_id=1, source_target_pairs={{0,1},{2,3},{4,5},{6,7},{8,9},{10,11},{12,13},{14,15},{16,17},{18,... | collective-permute-start | bytes 12296 | tf_op jit(solution)/shard_map/ppermute | solution.py:24
  20.6 4.7 %collective-permute-start.4 = (bf16[1,224,128]{2,1,0:T(8,128)(2,1)S(1)}, bf16[1,224,128]{2,1,0:T(8,128)(2,1)S(1)}, u32[]{:S(2)}, u32[]{:S(2)}) collective-permute-start(bf16[1,224,128]{2,1,0:T(8,128)(2,1)S(1)} %slice.284), channel_id=1, source_target_pairs={{0,30},{2,0},{4,2},{6,4},{8,6},{10,8},{12,10},{14,12},{16,14},{18,... | collective-permute-start | bytes 172040 | tf_op jit(solution)/shard_map/ppermute | solution.py:18
  23.5 5.5 %collective-permute-start.5 = (f32[8,1,128]{2,1,0:T(1,128)S(1)}, f32[8,1,128]{2,1,0:T(1,128)S(1)}, u32[]{:S(2)}, u32[]{:S(2)}) collective-permute-start(f32[8,1,128]{2,1,0:T(1,128)S(1)} %slice.192), channel_id=1, source_target_pairs={{1,0},{3,2},{5,4},{7,6},{9,8},{11,10},{13,12},{15,14},{17,16},{19,... | collective-permute-start | bytes 12296 | tf_op jit(solution)/shard_map/ppermute | solution.py:24
  29.0 7.3 %copy-start.3 = (bf16[8,224,128]{2,1,0:T(8,128)(2,1)S(1)}, bf16[8,224,128]{2,1,0:T(8,128)(2,1)}, u32[]{:S(2)}) copy-start(bf16[8,224,128]{2,1,0:T(8,128)(2,1)} %param.7) | copy-start | bytes 1376260
  29.9 6.5 %collective-permute-start.6 = (bf16[1,224,128]{2,1,0:T(8,128)(2,1)S(1)}, bf16[1,224,128]{2,1,0:T(8,128)(2,1)S(1)}, u32[]{:S(2)}, u32[]{:S(2)}) collective-permute-start(bf16[1,224,128]{2,1,0:T(8,128)(2,1)S(1)} %slice.283), channel_id=1, source_target_pairs={{0,2},{2,4},{4,6},{6,8},{8,10},{10,12},{12,14},{14,16},{16,18},{18... | collective-permute-start | bytes 172040 | tf_op jit(solution)/shard_map/ppermute | solution.py:18
  30.0 6.4 %collective-permute-start.7 = (f32[8,1,128]{2,1,0:T(1,128)S(1)}, f32[8,1,128]{2,1,0:T(1,128)S(1)}, u32[]{:S(2)}, u32[]{:S(2)}) collective-permute-start(f32[8,1,128]{2,1,0:T(1,128)S(1)} %slice.196), channel_id=1, source_target_pairs={{0,1},{2,3},{4,5},{6,7},{8,9},{10,11},{12,13},{14,15},{16,17},{18,... | collective-permute-start | bytes 12296 | tf_op jit(solution)/shard_map/ppermute | solution.py:24
  37.1 2.0 %collective-permute-start.8 = (bf16[1,224,128]{2,1,0:T(8,128)(2,1)S(1)}, bf16[1,224,128]{2,1,0:T(8,128)(2,1)S(1)}, u32[]{:S(2)}, u32[]{:S(2)}) collective-permute-start(bf16[1,224,128]{2,1,0:T(8,128)(2,1)S(1)} %slice.282), channel_id=1, source_target_pairs={{0,30},{2,0},{4,2},{6,4},{8,6},{10,8},{12,10},{14,12},{16,14},{18,... | collective-permute-start | bytes 172040 | tf_op jit(solution)/shard_map/ppermute | solution.py:18
  37.3 5.5 %collective-permute-start.9 = (f32[8,1,128]{2,1,0:T(1,128)S(1)}, f32[8,1,128]{2,1,0:T(1,128)S(1)}, u32[]{:S(2)}, u32[]{:S(2)}) collective-permute-start(f32[8,1,128]{2,1,0:T(1,128)S(1)} %slice.202), channel_id=1, source_target_pairs={{1,0},{3,2},{5,4},{7,6},{9,8},{11,10},{13,12},{15,14},{17,16},{19,... | collective-permute-start | bytes 12296 | tf_op jit(solution)/shard_map/ppermute | solution.py:24
  43.3 8.2 %collective-permute-start.11 = (f32[8,1,128]{2,1,0:T(1,128)S(1)}, f32[8,1,128]{2,1,0:T(1,128)S(1)}, u32[]{:S(2)}, u32[]{:S(2)}) collective-permute-start(f32[8,1,128]{2,1,0:T(1,128)S(1)} %slice.206), channel_id=1, source_target_pairs={{0,1},{2,3},{4,5},{6,7},{8,9},{10,11},{12,13},{14,15},{16,17},{18,... | collective-permute-start | bytes 12296 | tf_op jit(solution)/shard_map/ppermute | solution.py:24
  45.0 6.5 %collective-permute-start.10 = (bf16[1,224,128]{2,1,0:T(8,128)(2,1)S(1)}, bf16[1,224,128]{2,1,0:T(8,128)(2,1)S(1)}, u32[]{:S(2)}, u32[]{:S(2)}) collective-permute-start(bf16[1,224,128]{2,1,0:T(8,128)(2,1)S(1)} %slice.281), channel_id=1, source_target_pairs={{0,2},{2,4},{4,6},{6,8},{8,10},{10,12},{12,14},{14,16},{16,18},{18... | collective-permute-start | bytes 172040 | tf_op jit(solution)/shard_map/ppermute | solution.py:18
  52.6 1.9 %collective-permute-start.12 = (bf16[1,224,128]{2,1,0:T(8,128)(2,1)S(1)}, bf16[1,224,128]{2,1,0:T(8,128)(2,1)S(1)}, u32[]{:S(2)}, u32[]{:S(2)}) collective-permute-start(bf16[1,224,128]{2,1,0:T(8,128)(2,1)S(1)} %slice.280), channel_id=1, source_target_pairs={{0,30},{2,0},{4,2},{6,4},{8,6},{10,8},{12,10},{14,12},{16,14},{18,... | collective-permute-start | bytes 172040 | tf_op jit(solution)/shard_map/ppermute | solution.py:18
  52.6 5.5 %collective-permute-start.13 = (f32[8,1,128]{2,1,0:T(1,128)S(1)}, f32[8,1,128]{2,1,0:T(1,128)S(1)}, u32[]{:S(2)}, u32[]{:S(2)}) collective-permute-start(f32[8,1,128]{2,1,0:T(1,128)S(1)} %slice.213), channel_id=1, source_target_pairs={{1,0},{3,2},{5,4},{7,6},{9,8},{11,10},{13,12},{15,14},{17,16},{19,... | collective-permute-start | bytes 12296 | tf_op jit(solution)/shard_map/ppermute | solution.py:24
  58.7 8.0 %collective-permute-start.15 = (f32[8,1,128]{2,1,0:T(1,128)S(1)}, f32[8,1,128]{2,1,0:T(1,128)S(1)}, u32[]{:S(2)}, u32[]{:S(2)}) collective-permute-start(f32[8,1,128]{2,1,0:T(1,128)S(1)} %slice.217), channel_id=1, source_target_pairs={{0,1},{2,3},{4,5},{6,7},{8,9},{10,11},{12,13},{14,15},{16,17},{18,... | collective-permute-start | bytes 12296 | tf_op jit(solution)/shard_map/ppermute | solution.py:24
  60.4 6.4 %collective-permute-start.14 = (bf16[1,224,128]{2,1,0:T(8,128)(2,1)S(1)}, bf16[1,224,128]{2,1,0:T(8,128)(2,1)S(1)}, u32[]{:S(2)}, u32[]{:S(2)}) collective-permute-start(bf16[1,224,128]{2,1,0:T(8,128)(2,1)S(1)} %slice.279), channel_id=1, source_target_pairs={{0,2},{2,4},{4,6},{6,8},{8,10},{10,12},{12,14},{14,16},{16,18},{18... | collective-permute-start | bytes 172040 | tf_op jit(solution)/shard_map/ppermute | solution.py:18
where the time goes:
time: 69.1 us; the launch traced here: 68.7 us
  waiting for transfers between devices  27.1 us (39%)
  starting transfers between devices  23.2 us (34%)
  other arithmetic  10.9 us (16%)
  local copies, waits for them, and re-layouts  6.5 us (9%)
  between operations  1.1 us (2%)
    ppermute x8, waiting for transfers between devices, passed_along(): return lax.ppermute(value, axis, pairs)  16.1 us
    ppermute x8, starting transfers between devices, passed_along_2(): lax.ppermute(value, axis, [(source, source + steps) for source in range(l...  14.3 us
    ppermute x8, waiting for transfers between devices, passed_along_2(): lax.ppermute(value, axis, [(source, source + steps) for source in range(l...  11 us
    ppermute x8, starting transfers between devices, passed_along(): return lax.ppermute(value, axis, pairs)  8.81 us
    add x1, other arithmetic, body(): grad_kappa + kappa_term(gaps, concentration, nexts_first, north_open, upp...  3.13 us
    add x2, other arithmetic, retreat_faces(): return (adjoint + gained + (west_lon + west_lat + west_level), gaps)  3.02 us
    add x2, other arithmetic, advance_faces(): pair[0] * conc + pair[1] * nearby  1.68 us
  transfers between devices with their start and end apart: 16, of which 10 were waited for; matrix products, arithmetic and copies ran while one was open for 13% of the time, Pallas kernels for 0%

commit v1 on v0

v1 whole, which is shorter than its diff:
```python
import functools

import jax
import jax.numpy as jnp
from jax import lax
from jax.experimental import pallas as pl
from jax.experimental.pallas import tpu as pltpu
from jax.sharding import PartitionSpec as P

MESH = pl.DeviceIdType.MESH
PAD = 8
TILE = 16
F32 = jnp.float32
WEST, EAST, SOUTH, NORTH = 0, 1, 2, 3


def kernel(
    lons,
    lats,
    conc_in,
    wind_in,
    kappa_in,
    observed_in,
    grad_conc,
    grad_kappa,
    conc,
    middle,
    lam2,
    lam1,
    own0,
    oth0,
    own1,
    oth1,
    own2,
    oth2,
    wind,
    kappa,
    observed,
    lon_out,
    lon_in,
    lat_out,
    lat_in,
    row_in,
    face_out,
    face_in,
    load_sem,
    send_sem,
    recv_sem,
    early_send,
    early_recv,
):
    rows, cols, levels = conc_in.shape
    lon, lat = lax.axis_index("lon"), lax.axis_index("lat")
    places = (
        {"lon": lax.rem(lon + lons - 1, lons)},
        {"lon": lax.rem(lon + 1, lons)},
        {"lat": lax.rem(lat + lats - 1, lats)},
        {"lat": lax.rem(lat + 1, lats)},
    )
    loads = [
        pltpu.make_async_copy(
            conc_in, conc.at[pl.ds(1, rows), pl.ds(PAD, cols)], load_sem.at[0]
        ),
        pltpu.make_async_copy(kappa_in, kappa, load_sem.at[1]),
        pltpu.make_async_copy(wind_in, wind, load_sem.at[2]),
        pltpu.make_async_copy(observed_in, observed, load_sem.at[3]),
    ]
    for load in loads:
        load.start()

    barrier = pltpu.get_barrier_semaphore()
    for place in places:
        pl.semaphore_signal(barrier, inc=1, device_id=place, device_id_type=MESH)
    pl.semaphore_wait(barrier, 4)

    def remote(source, target, send, recv, place):
        copy = pltpu.make_async_remote_copy(
            src_ref=source,
            dst_ref=target,
            send_sem=send,
            recv_sem=recv,
            device_id=place,
            device_id_type=MESH,
        )
        copy.start()
        return copy

    started = []
    row_copies = [
        remote(
            wind_in.at[0, rows - 1], row_in.at[0], early_send.at[0], early_recv.at[0], places[EAST]
        ),
        remote(
            kappa_in.at[rows - 1], row_in.at[1], early_send.at[1], early_recv.at[1], places[EAST]
        ),
    ]
    started += row_copies

    def send_rims(state, turn):
        inner = pl.ds(PAD, cols)
        lon_out[turn, WEST] = state[1, inner].astype(jnp.bfloat16)
        lon_out[turn, EAST] = state[rows, inner].astype(jnp.bfloat16)
        for i in range(rows):
            lat_out[turn, 0, i : i + 1] = state[i + 1, PAD : PAD + 1]
            lat_out[turn, 1, i : i + 1] = state[i + 1, PAD + cols - 1 : PAD + cols]
        copies = []
        for way in (WEST, EAST):
            copies.append(
                remote(
                    lon_out.at[turn, way],
                    lon_in.at[turn, way],
                    send_sem.at[turn, way],
                    recv_sem.at[turn, way],
                    places[way],
                )
            )
        for way in (SOUTH, NORTH):
            copies.append(
                remote(
                    lat_out.at[turn, way - 2],
                    lat_in.at[turn, way - 2],
                    send_sem.at[turn, way],
                    recv_sem.at[turn, way],
                    places[way],
                )
            )
        started.extend(copies)
        return copies

    north_open = (lat < lats - 1).astype(F32)

    def take_rims(state, turn, copies):
        for copy in copies:
            copy.wait_recv()
        inner = pl.ds(PAD, cols)
        state[rows + 1, inner] = lon_in[turn, WEST].astype(F32)
        state[0, inner] = lon_in[turn, EAST].astype(F32)
        for i in range(rows):
            edge = state[i + 1, PAD + cols - 1 : PAD + cols]
            ghost = lat_in[turn, 0, i : i + 1]
            state[i + 1, PAD + cols : PAD + cols + 1] = edge + (ghost - edge) * north_open
            state[i + 1, PAD - 1 : PAD] = lat_in[turn, 1, i : i + 1]

    def pair(speed, diffuse):
        return jnp.maximum(speed, 0.0) + diffuse, jnp.minimum(speed, 0.0) - diffuse

    def upper(width):
        return (lax.broadcasted_iota(jnp.int32, (width, levels), 1) < levels - 1).astype(F32)

    def chunks(first, last, width, work):
        def one(t, carry):
            work(pl.multiple_of(first + t * width, width))
            return carry

        lax.fori_loop(0, (last - first) // width, one, 0)

    def up(value):
        return pltpu.roll(value, levels - 1, 1)

    def down(value):
        return pltpu.roll(value, 1, 1)

    loads[0].wait()
    copies = send_rims(conc, 0)

    loads[1].wait()
    loads[2].wait()

    def coefs_at(j):
        here = pl.ds(j, TILE)
        padded = pl.ds(pl.multiple_of(j + PAD, 8), TILE)
        shut = upper(TILE)
        for i in range(rows):
            diffuse = kappa[i, here].astype(F32)
            own, oth = pair(wind[0, i, here].astype(F32), diffuse)
            own0[i + 1, here] = own
            oth0[i + 1, here] = oth
            own, oth = pair(wind[1, i, here].astype(F32), diffuse)
            own1[i, padded] = own
            oth1[i, padded] = oth
            own, oth = pair(wind[2, i, here].astype(F32), diffuse)
            own2[i, here] = own * shut
            oth2[i, here] = oth * shut

    chunks(0, cols, TILE, coefs_at)
    last = PAD + cols - 1
    for i in range(rows):
        for place, table in enumerate((own1, oth1)):
            edge = table[i, last : last + 1] * north_open
            table[i, last : last + 1] = edge
            face_out[place, i : i + 1] = edge
    face_copy = remote(face_out, face_in, early_send.at[2], early_recv.at[2], places[NORTH])
    started.append(face_copy)

    def forward(state, target, minus, span, j, width):
        here = pl.ds(j, width)
        mid = pl.multiple_of(j + PAD, 8)
        at, south, north = pl.ds(mid, width), pl.ds(mid - 1, width), pl.ds(mid + 1, width)
        begin = span[0]
        c = state[begin + 1, at]
        f0_west = own0[begin, here] * state[begin, at] + oth0[begin, here] * c
        for i in span:
            east = state[i + 2, at]
            f0 = own0[i + 1, here] * c + oth0[i + 1, here] * east
            f1 = own1[i, at] * c + oth1[i, at] * state[i + 1, north]
            f1_south = own1[i, south] * state[i + 1, south] + oth1[i, south] * c
            f2 = own2[i, here] * c + oth2[i, here] * up(c)
            new = c - (f0 + f1 + f2) + (f0_west + f1_south + down(f2))
            if minus is not None:
                new = new - minus[i, here].astype(F32)
            target[i + 1, at] = new
            f0_west = f0
            c = east

    def backward(state, c_state, target, lead, add, span, j, width):
        here = pl.ds(j, width)
        mid = pl.multiple_of(j + PAD, 8)
        at, south, north = pl.ds(mid, width), pl.ds(mid - 1, width), pl.ds(mid + 1, width)
        spot = here if lead == 0 else at
        shut = upper(width)
        begin = span[0]
        lam = state[begin + 1, at]
        c = c_state[begin + 1, at]
        q0_west = oth0[begin, here] * (lam - state[begin, at])
        for i in span:
            lam_east, c_east = state[i + 2, at], c_state[i + 2, at]
            g0 = lam_east - lam
            g1 = state[i + 1, north] - lam
            g2 = up(lam) - lam
            k = g0 * (c - c_east) + g1 * (c - c_state[i + 1, north]) + g2 * (c - up(c)) * shut
            grad_kappa[i, here] = grad_kappa[i, here] + k if add else k
            gained = own0[i + 1, here] * g0 + own1[i, at] * g1 + own2[i, here] * g2
            q1_south = oth1[i, south] * (lam - state[i + 1, south])
            q2 = oth2[i, here] * g2
            target[i + lead, spot] = lam + gained + (q0_west + q1_south + down(q2))
            q0_west = oth0[i + 1, here] * g0
            lam, c = lam_east, c_east

    inside = tuple(range(1, rows - 1))

    def interior(step):
        chunks(TILE, cols - TILE, TILE, lambda j: step(inside, j, TILE))

    def rim(step):
        def ends(j):
            step((0,), j, TILE)
            step((rows - 1,), j, TILE)

        chunks(0, cols, TILE, ends)
        chunks(0, 2, 1, lambda t: step(inside, pl.multiple_of(t * (cols - TILE), TILE), TILE))

    first = functools.partial(forward, conc, middle, None)
    second = functools.partial(forward, middle, lam2, observed)
    third = functools.partial(backward, lam2, middle, lam1, 1, False)
    fourth = functools.partial(backward, lam1, conc, grad_conc, 0, True)

    interior(first)
    for copy in row_copies + [face_copy]:
        copy.wait_recv()
    own, oth = pair(row_in[0].astype(F32), row_in[1].astype(F32))
    own0[0] = own
    oth0[0] = oth
    for i in range(rows):
        own1[i, PAD - 1 : PAD] = face_in[0, i : i + 1]
        oth1[i, PAD - 1 : PAD] = face_in[1, i : i + 1]
    take_rims(conc, 0, copies)
    rim(first)

    copies = send_rims(middle, 1)
    loads[3].wait()
    interior(second)
    take_rims(middle, 1, copies)
    rim(second)

    copies = send_rims(lam2, 2)
    interior(third)
    take_rims(lam2, 2, copies)
    rim(third)

    copies = send_rims(lam1, 3)
    interior(fourth)
    take_rims(lam1, 3, copies)
    rim(fourth)

    for copy in started:
        copy.wait_send()


def body(lons, lats, concentration, wind, kappa, observed):
    rows, cols, levels = concentration.shape
    state = pltpu.VMEM((rows + 2, cols + 2 * PAD, levels), F32)
    padded = pltpu.VMEM((rows, cols + 2 * PAD, levels), F32)
    wider = pltpu.VMEM((rows + 1, cols, levels), F32)
    plain = pltpu.VMEM((rows, cols, levels), F32)
    out = jax.ShapeDtypeStruct(concentration.shape, F32)
    return pl.pallas_call(
        functools.partial(kernel, lons, lats),
        out_shape=(out, out),
        in_specs=[pl.BlockSpec(memory_space=pl.ANY)] * 4,
        out_specs=(pl.BlockSpec(memory_space=pltpu.VMEM),) * 2,
        scratch_shapes=[
            state,
            state,
            state,
            state,
            wider,
            wider,
            padded,
            padded,
            plain,
            plain,
            pltpu.VMEM(wind.shape, wind.dtype),
            pltpu.VMEM(kappa.shape, kappa.dtype),
            pltpu.VMEM(observed.shape, observed.dtype),
            pltpu.VMEM((4, 2, cols, levels), jnp.bfloat16),
            pltpu.VMEM((4, 2, cols, levels), jnp.bfloat16),
            pltpu.VMEM((4, 2, rows, levels), F32),
            pltpu.VMEM((4, 2, rows, levels), F32),
            pltpu.VMEM((2, cols, levels), jnp.bfloat16),
            pltpu.VMEM((2, rows, levels), F32),
            pltpu.VMEM((2, rows, levels), F32),
            pltpu.SemaphoreType.DMA((4,)),
            pltpu.SemaphoreType.DMA((4, 4)),
            pltpu.SemaphoreType.DMA((4, 4)),
            pltpu.SemaphoreType.DMA((3,)),
            pltpu.SemaphoreType.DMA((3,)),
        ],
        compiler_params=pltpu.CompilerParams(
            collective_id=0, has_side_effects=True, vmem_limit_bytes=60 * 1024 * 1024
        ),
    )(concentration, wind, kappa, observed)


def solution(mesh):
    lons, lats = mesh.shape["lon"], mesh.shape["lat"]
    return jax.shard_map(
        functools.partial(body, lons, lats),
        mesh=mesh,
        in_specs=(
            P("lon", "lat", None),
            P(None, "lon", "lat", None),
            P("lon", "lat", None),
            P("lon", "lat", None),
        ),
        out_specs=(P("lon", "lat", None), P("lon", "lat", None)),
        check_vma=False,
    )
```

time: 69.1 us -> 37 us (0.54)
  Pallas kernels: 0 us -> 33.1 us
  waiting for transfers between devices: 27.1 us -> 0 us
  starting transfers between devices: 23.2 us -> 0 us
  other arithmetic: 10.9 us -> 0 us
  local copies, waits for them, and re-layouts: 6.5 us -> 3.17 us
    pallas_call x0 -> x1, Pallas kernels: none -> 33.1 us  [body(): pl.pallas_call(functools.partial(kernel, lons, lats), out_shape=(out, out...]
    ppermute x16 -> x0, waiting for transfers between devices: 27.1 us -> none  [the longest x8 16.1 us: passed_along(): return lax.ppermute(value, axis, pairs)]
    ppermute x16 -> x0, starting transfers between devices: 23.2 us -> none  [the longest x8 14.3 us: passed_along_2(): lax.ppermute(value, axis, [(source, source + steps) for source in range(l...]
    add x6 -> x0, other arithmetic: 8.49 us -> none  [the longest x1 3.13 us: body(): grad_kappa + kappa_term(gaps, concentration, nexts_first, north_open, upp...]
    slice x32 -> x0, local copies, waits for them, and re-layouts: 6.13 us -> none  [the longest x2 1.31 us: advance_faces(): conc[:, 1:]]
    unnamed x8 -> x4, local copies, waits for them, and re-layouts: 0.37 us -> 3.17 us
    mul x4 -> x0, other arithmetic: 1.31 us -> none  [retreat_faces(): parts = tuple((pair[1] * gap for pair, gap in zip(table, gaps)))]
    sub x1 -> x0, other arithmetic: 0.69 us -> none  [body(): adjoint = final - observed.astype(jnp.float32)]
  transfers between devices with their start and end apart: 16 -> 0, of which waited for: 10 -> 0; matrix products, arithmetic and copies ran while one was open for 13% -> 0% of each run, Pallas kernels for 0% -> 0%
where the time goes in v1:
time: 37 us; the launch traced here: 36.9 us
  Pallas kernels  33.1 us (89%)
  local copies, waits for them, and re-layouts  3.17 us (9%)
  between operations  0.65 us (2%)
    pallas_call x1, Pallas kernels, body(): pl.pallas_call(functools.partial(kernel, lons, lats), out_shape=(out, out...  33.1 us
    unnamed x4, local copies, waits for them, and re-layouts  3.17 us

profile of v1, /device:TPU:0, one launch (start us, length us, event | category | flops | bytes accessed | tf_op | source)
XLA Modules:
  0.0 36.9 jit_solution(17327109482658483643)
XLA Ops:
  0.6 33.1 %shard_map.59 = (f32[8,224,128]{2,1,0:T(8,128)}, f32[8,224,128]{2,1,0:T(8,128)}) custom-call(f32[8,224,128]{2,1,0:T(8,128)} %conc_in.1, bf16[3,8,224,128]{3,2,1,0:T(8,128)(2,1)} %wind_in.1, bf16[8,224,128]{2,1,0:T(8,128)(2,1)} %kappa_in.1, bf16[8,224,128]{2,1,0:T(8,128)(2,1)} %observed_in.1), custom_call_target="tpu_custom_call" | custom-call | tf_op jit(solution)/shard_map/pallas_call | solution.py:296
  33.7 0.0 copy-start
  33.7 2.2 %copy.8 = f32[8,224,128]{2,1,0:T(8,128)} copy(f32[8,224,128]{2,1,0:T(8,128)} %get-tuple-element.4) | data formatting | bytes 1835008
  36.0 0.0 copy-done
  36.0 0.9 %copy.9 = f32[8,224,128]{2,1,0:T(8,128)} copy(f32[8,224,128]{2,1,0:T(8,128)S(1)} %copy-done) | data formatting | bytes 1835008
Async XLA Ops:
  33.7 2.3 %copy-start = (f32[8,224,128]{2,1,0:T(8,128)S(1)}, f32[8,224,128]{2,1,0:T(8,128)}, u32[]{:S(2)}) copy-start(f32[8,224,128]{2,1,0:T(8,128)} %get-tuple-element.5) | copy-start | bytes 2752516

commit v2 on v1

--- a/solution.py
+++ b/solution.py
@@ -44,8 +44,10 @@
     face_out,
     face_in,
     load_sem,
-    send_sem,
-    recv_sem,
+    lon_send,
+    lon_recv,
+    lat_send,
+    lat_recv,
     early_send,
     early_recv,
 ):
@@ -96,45 +98,54 @@
     ]
     started += row_copies
 
-    def send_rims(state, turn):
-        inner = pl.ds(PAD, cols)
-        lon_out[turn, WEST] = state[1, inner].astype(jnp.bfloat16)
-        lon_out[turn, EAST] = state[rows, inner].astype(jnp.bfloat16)
-        for i in range(rows):
-            lat_out[turn, 0, i : i + 1] = state[i + 1, PAD : PAD + 1]
-            lat_out[turn, 1, i : i + 1] = state[i + 1, PAD + cols - 1 : PAD + cols]
+    half = cols // 2
+
+    def send_lon(state, turn, part):
+        inner, there = pl.ds(PAD + part * half, half), pl.ds(part * half, half)
         copies = []
-        for way in (WEST, EAST):
+        for way, row in ((EAST, rows), (WEST, 1)):
+            lon_out[turn, way, there] = state[row, inner].astype(jnp.bfloat16)
             copies.append(
                 remote(
-                    lon_out.at[turn, way],
-                    lon_in.at[turn, way],
-                    send_sem.at[turn, way],
-                    recv_sem.at[turn, way],
-                    places[way],
-                )
-            )
-        for way in (SOUTH, NORTH):
-            copies.append(
-                remote(
-                    lat_out.at[turn, way - 2],
-                    lat_in.at[turn, way - 2],
-                    send_sem.at[turn, way],
-                    recv_sem.at[turn, way],
+                    lon_out.at[turn, way, there],
+                    lon_in.at[turn, way, there],
+                    lon_send.at[turn, way, part],
+                    lon_recv.at[turn, way, part],
                     places[way],
                 )
             )
         started.extend(copies)
         return copies
 
+    def send_lat(state, turn):
+        copies = []
+        for way, col in ((SOUTH, PAD), (NORTH, PAD + cols - 1)):
+            for i in range(rows):
+                lat_out[turn, way - 2, i : i + 1] = state[i + 1, col : col + 1]
+            copies.append(
+                remote(
+                    lat_out.at[turn, way - 2],
+                    lat_in.at[turn, way - 2],
+                    lat_send.at[turn, way - 2],
+                    lat_recv.at[turn, way - 2],
+                    places[way],
+                )
+            )
+        started.extend(copies)
+        return copies
+
     north_open = (lat < lats - 1).astype(F32)
 
-    def take_rims(state, turn, copies):
+    def take_lon(state, turn, part, copies):
         for copy in copies:
             copy.wait_recv()
-        inner = pl.ds(PAD, cols)
-        state[rows + 1, inner] = lon_in[turn, WEST].astype(F32)
-        state[0, inner] = lon_in[turn, EAST].astype(F32)
+        inner, there = pl.ds(PAD + part * half, half), pl.ds(part * half, half)
+        state[rows + 1, inner] = lon_in[turn, WEST, there].astype(F32)
+        state[0, inner] = lon_in[turn, EAST, there].astype(F32)
+
+    def take_lat(state, turn, copies):
+        for copy in copies:
+            copy.wait_recv()
         for i in range(rows):
             edge = state[i + 1, PAD + cols - 1 : PAD + cols]
             ghost = lat_in[turn, 0, i : i + 1]
@@ -144,15 +155,26 @@
     def pair(speed, diffuse):
         return jnp.maximum(speed, 0.0) + diffuse, jnp.minimum(speed, 0.0) - diffuse
 
+    def aligned(start):
+        return start if isinstance(start, int) else pl.multiple_of(start, 8)
+
     def upper(width):
         return (lax.broadcasted_iota(jnp.int32, (width, levels), 1) < levels - 1).astype(F32)
 
-    def chunks(first, last, width, work):
+    def chunks(first, last, width, work, most):
+        count = (last - first) // width
+        group = max(g for g in range(1, most + 1) if count % g == 0)
+
         def one(t, carry):
-            work(pl.multiple_of(first + t * width, width))
+            for g in range(group):
+                work(pl.multiple_of(first + (t * group + g) * width, width))
             return carry
 
-        lax.fori_loop(0, (last - first) // width, one, 0)
+        if count == group:
+            for g in range(group):
+                work(first + g * width)
+        else:
+            lax.fori_loop(0, count // group, one, 0)
 
     def up(value):
         return pltpu.roll(value, levels - 1, 1)
@@ -161,14 +183,15 @@
         return pltpu.roll(value, 1, 1)
 
     loads[0].wait()
-    copies = send_rims(conc, 0)
+    lon_copies = [send_lon(conc, 0, part) for part in (0, 1)]
+    lat_copies = send_lat(conc, 0)
 
     loads[1].wait()
     loads[2].wait()
 
     def coefs_at(j):
         here = pl.ds(j, TILE)
-        padded = pl.ds(pl.multiple_of(j + PAD, 8), TILE)
+        padded = pl.ds(aligned(j + PAD), TILE)
         shut = upper(TILE)
         for i in range(rows):
             diffuse = kappa[i, here].astype(F32)
@@ -182,7 +205,7 @@
             own2[i, here] = own * shut
             oth2[i, here] = oth * shut
 
-    chunks(0, cols, TILE, coefs_at)
+    chunks(0, cols, TILE, coefs_at, 2)
     last = PAD + cols - 1
     for i in range(rows):
         for place, table in enumerate((own1, oth1)):
@@ -194,7 +217,7 @@
 
     def forward(state, target, minus, span, j, width):
         here = pl.ds(j, width)
-        mid = pl.multiple_of(j + PAD, 8)
+        mid = aligned(j + PAD)
         at, south, north = pl.ds(mid, width), pl.ds(mid - 1, width), pl.ds(mid + 1, width)
         begin = span[0]
         c = state[begin + 1, at]
@@ -214,7 +237,7 @@
 
     def backward(state, c_state, target, lead, add, span, j, width):
         here = pl.ds(j, width)
-        mid = pl.multiple_of(j + PAD, 8)
+        mid = aligned(j + PAD)
         at, south, north = pl.ds(mid, width), pl.ds(mid - 1, width), pl.ds(mid + 1, width)
         spot = here if lead == 0 else at
         shut = upper(width)
@@ -239,15 +262,18 @@
     inside = tuple(range(1, rows - 1))
 
     def interior(step):
-        chunks(TILE, cols - TILE, TILE, lambda j: step(inside, j, TILE))
-
-    def rim(step):
-        def ends(j):
+        chunks(TILE, cols - TILE, TILE, lambda j: step(inside, j, TILE), 4)
+
+    def sides(step):
+        step(inside, 0, TILE)
+        step(inside, cols - TILE, TILE)
+
+    def ends(step, part):
+        def both(j):
             step((0,), j, TILE)
             step((rows - 1,), j, TILE)
 
-        chunks(0, cols, TILE, ends)
-        chunks(0, 2, 1, lambda t: step(inside, pl.multiple_of(t * (cols - TILE), TILE), TILE))
+        chunks(part * half, (part + 1) * half, TILE, both, 7)
 
     first = functools.partial(forward, conc, middle, None)
     second = functools.partial(forward, middle, lam2, observed)
@@ -255,32 +281,35 @@
     fourth = functools.partial(backward, lam1, conc, grad_conc, 0, True)
 
     interior(first)
-    for copy in row_copies + [face_copy]:
+    face_copy.wait_recv()
+    for i in range(rows):
+        own1[i, PAD - 1 : PAD] = face_in[0, i : i + 1]
+        oth1[i, PAD - 1 : PAD] = face_in[1, i : i + 1]
+    take_lat(conc, 0, lat_copies)
+    sides(first)
+    for copy in row_copies:
         copy.wait_recv()
     own, oth = pair(row_in[0].astype(F32), row_in[1].astype(F32))
     own0[0] = own
     oth0[0] = oth
-    for i in range(rows):
-        own1[i, PAD - 1 : PAD] = face_in[0, i : i + 1]
-        oth1[i, PAD - 1 : PAD] = face_in[1, i : i + 1]
-    take_rims(conc, 0, copies)
-    rim(first)
-
-    copies = send_rims(middle, 1)
-    loads[3].wait()
-    interior(second)
-    take_rims(middle, 1, copies)
-    rim(second)
-
-    copies = send_rims(lam2, 2)
-    interior(third)
-    take_rims(lam2, 2, copies)
-    rim(third)
-
-    copies = send_rims(lam1, 3)
-    interior(fourth)
-    take_rims(lam1, 3, copies)
-    rim(fourth)
+    for part in (0, 1):
+        take_lon(conc, 0, part, lon_copies[part])
+        ends(first, part)
+        lon_copies[part] = send_lon(middle, 1, part)
+
+    turns = ((middle, second), (lam2, third), (lam1, fourth))
+    for turn, (state, step) in enumerate(turns, 1):
+        lat_copies = send_lat(state, turn)
+        if turn == 1:
+            loads[3].wait()
+        interior(step)
+        take_lat(state, turn, lat_copies)
+        sides(step)
+        for part in (0, 1):
+            take_lon(state, turn, part, lon_copies[part])
+            ends(step, part)
+            if turn < 3:
+                lon_copies[part] = send_lon(turns[turn][0], turn + 1, part)
 
     for copy in started:
         copy.wait_send()
@@ -293,7 +322,7 @@
     wider = pltpu.VMEM((rows + 1, cols, levels), F32)
     plain = pltpu.VMEM((rows, cols, levels), F32)
     out = jax.ShapeDtypeStruct(concentration.shape, F32)
-    return pl.pallas_call(
+    results = pl.pallas_call(
         functools.partial(kernel, lons, lats),
         out_shape=(out, out),
         in_specs=[pl.BlockSpec(memory_space=pl.ANY)] * 4,
@@ -320,8 +349,10 @@
             pltpu.VMEM((2, rows, levels), F32),
             pltpu.VMEM((2, rows, levels), F32),
             pltpu.SemaphoreType.DMA((4,)),
-            pltpu.SemaphoreType.DMA((4, 4)),
-            pltpu.SemaphoreType.DMA((4, 4)),
+            pltpu.SemaphoreType.DMA((4, 2, 2)),
+            pltpu.SemaphoreType.DMA((4, 2, 2)),
+            pltpu.SemaphoreType.DMA((4, 2)),
+            pltpu.SemaphoreType.DMA((4, 2)),
             pltpu.SemaphoreType.DMA((3,)),
             pltpu.SemaphoreType.DMA((3,)),
         ],
@@ -329,6 +360,20 @@
             collective_id=0, has_side_effects=True, vmem_limit_bytes=60 * 1024 * 1024
         ),
     )(concentration, wind, kappa, observed)
+
+    def hand_over(conc_from, kappa_from, conc_to, kappa_to):
+        conc_to[...] = conc_from[...]
+        kappa_to[...] = kappa_from[...]
+
+    block = pl.BlockSpec((4, cols, levels), lambda i: (i, 0, 0))
+    return pl.pallas_call(
+        hand_over,
+        grid=(rows // 4,),
+        out_shape=(out, out),
+        in_specs=[block] * 2,
+        out_specs=(block,) * 2,
+        compiler_params=pltpu.CompilerParams(vmem_limit_bytes=60 * 1024 * 1024),
+    )(*results)
 
 
 def solution(mesh):

time: 37 us -> 26.7 us (0.72)
  Pallas kernels: 33.1 us -> 25.9 us
  local copies, waits for them, and re-layouts: 3.17 us -> 0 us
    pallas_call x1, Pallas kernels: 33.1 us -> 23.5 us  [body(): pl.pallas_call(functools.partial(kernel, lons, lats), out_shape=(out, out...]
    unnamed x4 -> x0, local copies, waits for them, and re-layouts: 3.17 us -> none
    pallas_call x0 -> x1, Pallas kernels: none -> 2.45 us  [body(): pl.pallas_call(hand_over, grid=(rows // 4,), out_shape=(out, out), in_spe...]
where the time goes in v2:
time: 26.7 us; the launch traced here: 26.5 us
  Pallas kernels  25.9 us (97%)
  between operations  0.64 us (2%)
    pallas_call x1, Pallas kernels, body(): pl.pallas_call(functools.partial(kernel, lons, lats), out_shape=(out, out...  23.5 us
    pallas_call x1, Pallas kernels, body(): pl.pallas_call(hand_over, grid=(rows // 4,), out_shape=(out, out), in_spe...  2.45 us

profile of v2, /device:TPU:0, one launch (start us, length us, event | category | flops | bytes accessed | tf_op | source)
XLA Modules:
  0.0 26.5 jit_solution(6133741853996351312)
XLA Ops:
  0.6 23.5 %shard_map.59 = (f32[8,224,128]{2,1,0:T(8,128)}, f32[8,224,128]{2,1,0:T(8,128)}) custom-call(f32[8,224,128]{2,1,0:T(8,128)} %conc_in.1, bf16[3,8,224,128]{3,2,1,0:T(8,128)(2,1)} %wind_in.1, bf16[8,224,128]{2,1,0:T(8,128)(2,1)} %kappa_in.1, bf16[8,224,128]{2,1,0:T(8,128)(2,1)} %observed_in.1), custom_call_target="tpu_custom_call" | custom-call | tf_op jit(solution)/shard_map/pallas_call | solution.py:325
  24.1 2.5 %shard_map.60 = (f32[8,224,128]{2,1,0:T(8,128)}, f32[8,224,128]{2,1,0:T(8,128)}) custom-call(f32[8,224,128]{2,1,0:T(8,128)} %get-tuple-element.4.conc_from, f32[8,224,128]{2,1,0:T(8,128)} %get-tuple-element.5.kappa_from), custom_call_target="tpu_custom_call" | custom-call | tf_op jit(solution)/shard_map/pallas_call | solution.py:369

commit v3 on v2

--- a/solution.py
+++ b/solution.py
@@ -21,6 +21,8 @@
     wind_in,
     kappa_in,
     observed_in,
+    conc_to,
+    kappa_to,
     grad_conc,
     grad_kappa,
     conc,
@@ -50,6 +52,7 @@
     lat_recv,
     early_send,
     early_recv,
+    store_sem,
 ):
     rows, cols, levels = conc_in.shape
     lon, lat = lax.axis_index("lon"), lax.axis_index("lat")
@@ -280,6 +283,17 @@
     third = functools.partial(backward, lam2, middle, lam1, 1, False)
     fourth = functools.partial(backward, lam1, conc, grad_conc, 0, True)
 
+    stores = []
+
+    def store(row, count, col, width, slot):
+        where = (pl.ds(row, count), pl.ds(col, width))
+        for n, (source, target) in enumerate(((grad_conc, conc_to), (grad_kappa, kappa_to))):
+            copy = pltpu.make_async_copy(
+                source.at[where], target.at[where], store_sem.at[n, slot]
+            )
+            copy.start()
+            stores.append(copy)
+
     interior(first)
     face_copy.wait_recv()
     for i in range(rows):
@@ -305,12 +319,19 @@
         interior(step)
         take_lat(state, turn, lat_copies)
         sides(step)
+        if turn == 3:
+            store(1, rows - 2, 0, cols, 0)
         for part in (0, 1):
             take_lon(state, turn, part, lon_copies[part])
             ends(step, part)
-            if turn < 3:
+            if turn == 3:
+                store(0, 1, part * half, half, 1 + part)
+                store(rows - 1, 1, part * half, half, 3 + part)
+            else:
                 lon_copies[part] = send_lon(turns[turn][0], turn + 1, part)
 
+    for copy in stores:
+        copy.wait()
     for copy in started:
         copy.wait_send()
 
@@ -326,8 +347,10 @@
         functools.partial(kernel, lons, lats),
         out_shape=(out, out),
         in_specs=[pl.BlockSpec(memory_space=pl.ANY)] * 4,
-        out_specs=(pl.BlockSpec(memory_space=pltpu.VMEM),) * 2,
+        out_specs=(pl.BlockSpec(memory_space=pl.ANY),) * 2,
         scratch_shapes=[
+            plain,
+            plain,
             state,
             state,
             state,
@@ -355,6 +378,7 @@
             pltpu.SemaphoreType.DMA((4, 2)),
             pltpu.SemaphoreType.DMA((3,)),
             pltpu.SemaphoreType.DMA((3,)),
+            pltpu.SemaphoreType.DMA((2, 5)),
         ],
         compiler_params=pltpu.CompilerParams(
             collective_id=0, has_side_effects=True, vmem_limit_bytes=60 * 1024 * 1024

time: 26.7 us -> 26.2 us (0.981)
  Pallas kernels: 25.9 us -> 25.4 us
    pallas_call x1, Pallas kernels: 23.5 us -> 23 us  [body(): pl.pallas_call(functools.partial(kernel, lons, lats), out_shape=(out, out...]
where the time goes in v3:
time: 26.2 us; the launch traced here: 26.1 us
  Pallas kernels  25.4 us (97%)
  between operations  0.64 us (2%)
    pallas_call x1, Pallas kernels, body(): pl.pallas_call(functools.partial(kernel, lons, lats), out_shape=(out, out...  23 us
    pallas_call x1, Pallas kernels, body(): pl.pallas_call(hand_over, grid=(rows // 4,), out_shape=(out, out), in_spe...  2.45 us

profile of v3, /device:TPU:0, one launch (start us, length us, event | category | flops | bytes accessed | tf_op | source)
XLA Modules:
  0.0 26.1 jit_solution(8107057453870250883)
XLA Ops:
  0.6 23.0 %shard_map.59 = (f32[8,224,128]{2,1,0:T(8,128)}, f32[8,224,128]{2,1,0:T(8,128)}) custom-call(f32[8,224,128]{2,1,0:T(8,128)} %conc_in.1, bf16[3,8,224,128]{3,2,1,0:T(8,128)(2,1)} %wind_in.1, bf16[8,224,128]{2,1,0:T(8,128)(2,1)} %kappa_in.1, bf16[8,224,128]{2,1,0:T(8,128)(2,1)} %observed_in.1), custom_call_target="tpu_custom_call" | custom-call | tf_op jit(solution)/shard_map/pallas_call | solution.py:346
  23.6 2.5 %shard_map.60 = (f32[8,224,128]{2,1,0:T(8,128)}, f32[8,224,128]{2,1,0:T(8,128)}) custom-call(f32[8,224,128]{2,1,0:T(8,128)} %get-tuple-element.4.conc_from, f32[8,224,128]{2,1,0:T(8,128)} %get-tuple-element.5.kappa_from), custom_call_target="tpu_custom_call" | custom-call | tf_op jit(solution)/shard_map/pallas_call | solution.py:393
